TPU v7x, 32 devices: a whole 2x2x4 slice. The times are simulated.
32 devices in a mesh: pop: 8 (over z, x), tensor: 4 (over y, core).
Axes of the slice: x: 2, y: 2, z: 4, core: 2. Of those that a mesh axis runs over, the one named last changes fastest.
Arguments:
- token_ids: int32 [64, 64], P('pop'), may hold values from 0 to 76031, as said below
- ranks: int32 [64], P('pop'), may hold values from 0 to 63, each once
- embed_table: bfloat16 [76032, 3584], P('pop', 'tensor'), may hold values from -6 to 6
- norm_gain: bfloat16 [3584], replicated, may hold values from 0.5 to 1.5
- gate_weight: bfloat16 [3584, 18944], P('pop', 'tensor'), may hold values from -0.09375 to 0.09375
- up_weight: bfloat16 [3584, 18944], P('pop', 'tensor'), may hold values from -0.09375 to 0.09375
- gate_left: bfloat16 [64, 3584], P('pop'), may hold values from -6 to 6
- up_left: bfloat16 [64, 3584], P('pop'), may hold values from -6 to 6
- gate_right: bfloat16 [64, 18944], P('pop', 'tensor'), may hold values from -6 to 6
- up_right: bfloat16 [64, 18944], P('pop', 'tensor'), may hold values from -6 to 6
Outputs:
- hidden: bfloat16 [4096, 18944], P('pop', 'tensor')
- gate_step: float32 [3584, 18944], P('pop', 'tensor')
- up_step: float32 [3584, 18944], P('pop', 'tensor')
Inputs may be any that keep to these rules, and one draw needn't show every extreme that they name: Split token_ids into aligned blocks of 8 members (the members of one index of pop) and the table into blocks of 9504 rows: in every block of members, at most 128 ids fall in any one block of table rows, and exactly 128 in one of them.
All inputs are finite; a program needn't handle non-finite values.
Results may differ from a plain program's by a relative error of at most 0.0058.
Values may be sent and summed in bfloat16 or wider, within the bound.
A program may use at most 256 MiB of HBM per device.

v0:
```python
import math

import jax
import jax.numpy as jnp
from jax import lax
from jax.sharding import PartitionSpec as P


def split_high(x):
    high = lax.reduce_precision(x, exponent_bits=8, mantissa_bits=7)
    low = x - high
    return jnp.concatenate([high.astype(jnp.bfloat16), low.astype(jnp.bfloat16)], axis=0)


def weighted_step(left, right, score):
    scaled = split_high(left.astype(jnp.float32) * score[:, None])
    both = jnp.concatenate([right, right], axis=0)
    return lax.dot_general(
        scaled, both, (((0,), (0,)), ((), ())), preferred_element_type=jnp.float32
    )


def per_device(
    token_ids,
    ranks,
    embed_table,
    norm_gain,
    gate_weight,
    up_weight,
    gate_left,
    up_left,
    gate_right,
    up_right,
):
    pops = lax.axis_size("pop")
    pop = lax.axis_index("pop")
    tensor = lax.axis_index("tensor")
    table_rows, features = embed_table.shape
    own_members, prompt = token_ids.shape
    row_count, hidden_cols = gate_weight.shape
    width = norm_gain.shape[0]
    members = own_members * pops
    part = -(-hidden_cols // (128 * pops)) * 128
    padded = part * pops

    def pad_cols(x):
        return jnp.pad(x, ((0, 0), (0, padded - hidden_cols)))

    all_ids = lax.all_gather(token_ids, "pop", axis=0, tiled=True)
    all_ranks = lax.all_gather(ranks, "pop", axis=0, tiled=True)
    local_ids = all_ids.reshape(-1) - pop * table_rows
    owned = (local_ids >= 0) & (local_ids < table_rows)
    picked = jnp.take(embed_table, jnp.clip(local_ids, 0, table_rows - 1), axis=0)
    partial_rows = jnp.where(owned[:, None], picked, jnp.bfloat16(0))
    own_cols = lax.psum_scatter(partial_rows, "pop", scatter_dimension=0, tiled=True)

    gate_cols = lax.all_to_all(pad_cols(gate_weight), "pop", 1, 0, tiled=True)
    up_cols = lax.all_to_all(pad_cols(up_weight), "pop", 1, 0, tiled=True)

    values = own_cols.astype(jnp.float32)
    total = lax.psum(jnp.sum(values * values, axis=-1), "tensor")
    gain = lax.dynamic_slice_in_dim(norm_gain, tensor * features, features, 0)
    own_normed = (
        values * lax.rsqrt(total[:, None] * (1.0 / width) + 1e-06) * gain.astype(jnp.float32)
    ).astype(jnp.bfloat16)
    some = lax.all_gather(own_normed, "pop", axis=0, tiled=True)
    normed = lax.all_gather(some, "tensor", axis=1, tiled=True)

    all_gl, all_ul, all_gr, all_ur = (
        lax.all_gather(gate_left, "pop", axis=0, tiled=True),
        lax.all_gather(up_left, "pop", axis=0, tiled=True),
        lax.all_gather(gate_right, "pop", axis=0, tiled=True),
        lax.all_gather(up_right, "pop", axis=0, tiled=True),
    )
    scale = 0.5 / math.sqrt(width)
    blocks = normed.reshape(members, prompt, width)

    def project(weight, left, right):
        base = jnp.dot(normed, weight, preferred_element_type=jnp.float32)
        side = jnp.einsum("mld,md->ml", blocks, left, preferred_element_type=jnp.float32) * scale
        cols = lax.dynamic_slice_in_dim(pad_cols(right), pop * part, part, 1)
        return (
            base.reshape(members, prompt, part)
            + side[:, :, None] * cols.astype(jnp.float32)[:, None, :]
        )

    gate = project(gate_cols, all_gl, all_gr)
    up = project(up_cols, all_ul, all_ur)
    mine = (jax.nn.silu(gate) * up).astype(jnp.bfloat16).reshape(members * prompt, part)
    hidden = lax.all_to_all(mine, "pop", 0, 1, tiled=True)[:, :hidden_cols]

    score = (2.0 * all_ranks.astype(jnp.float32) - (members - 1)) / (members - 1)
    score = score * (1.0 / math.sqrt(members))
    row_start = pop * row_count
    left_gate = lax.dynamic_slice_in_dim(all_gl, row_start, row_count, 1)
    left_up = lax.dynamic_slice_in_dim(all_ul, row_start, row_count, 1)
    gate_step = weighted_step(left_gate, all_gr, score)
    up_step = weighted_step(left_up, all_ur, score)
    return (hidden, gate_step, up_step)


def solution(mesh):
    in_specs = (
        P("pop", None),
        P("pop"),
        P("pop", "tensor"),
        P(),
        P("pop", "tensor"),
        P("pop", "tensor"),
        P("pop", None),
        P("pop", None),
        P("pop", "tensor"),
        P("pop", "tensor"),
    )
    out_specs = (P("pop", "tensor"), P("pop", "tensor"), P("pop", "tensor"))
    return jax.shard_map(
        per_device, mesh=mesh, in_specs=in_specs, out_specs=out_specs, check_vma=False
    )
```

profile of v0, /device:TPU:0, one launch (start us, length us, event | category | flops | bytes accessed | tf_op | source)
XLA Modules:
  0.0 799.4 jit_solution(13260142982139188664)
XLA Ops:
  7.2 32.3 %all_gather.24 = s32[64,64]{1,0:T(8,128)S(1)} all-gather(s32[8,64]{1,0:T(8,128)} %param.10), channel_id=1, replica_groups=mesh['pop'=8,'tensor'=4] {'pop'}, dimensions={0}, use_global_device_ids=true | all-gather | bytes 18432 | tf_op jit(solution)/shard_map/all_gather | solution.py:49
  39.9 27.8 %gather_fusion = bf16[4096,896]{1,0:T(8,128)(2,1)} fusion(bf16[9504,896]{1,0:T(8,128)(2,1)} %param.12, s32[4096]{0:T(1024)S(1)} %broadcast_clamp_fusion), kind=kCustom, calls=%fused_computation | custom fusion | bytes 14696448 | tf_op jit(solution)/shard_map/jit(_take)/gather | solution.py:53
  67.7 7.0 select_select_fusion
  75.5 132.9 %reduce-scatter.2.cloned.1.call-done = bf16[512,896]{1,0:T(8,128)(2,1)} async-done(((bf16[4096,896]{1,0:T(8,128)(2,1)}), bf16[512,896]{1,0:T(8,128)(2,1)}) %reduce-scatter.2.cloned.1.call-update) | async-done | bytes 917520 | tf_op jit(solution)/shard_map/reduce_scatter | solution.py:55
  209.9 5.7 psum.7
  218.0 111.5 %all-gather.3.cloned.1.call-done = bf16[4096,896]{1,0:T(8,128)(2,1)} async-done(((bf16[512,896]{1,0:T(8,128)(2,1)}), bf16[4096,896]{1,0:T(8,128)(2,1)}) %all-gather.3.cloned.1.call-update) | async-done | bytes 7340048 | tf_op jit(solution)/shard_map/all_gather | solution.py:66
  334.9 4.8 all-to-all-start
  339.7 4.0 pad.16
  343.7 3.2 copy.29
  346.9 115.7 %all_gather.28 = bf16[64,4736]{1,0:T(8,128)(2,1)S(1)} all-gather(bf16[8,4736]{1,0:T(8,128)(2,1)S(1)} %copy-done), channel_id=1, replica_groups=mesh['pop'=8,'tensor'=4] {'pop'}, dimensions={0}, use_global_device_ids=true | all-gather | bytes 681984 | tf_op jit(solution)/shard_map/all_gather | solution.py:72
  462.7 31.8 %all_gather.30 = bf16[64,4736]{1,0:T(8,128)(2,1)S(1)} all-gather(bf16[8,4736]{1,0:T(8,128)(2,1)S(1)} %copy-done.1), channel_id=1, replica_groups=mesh['pop'=8,'tensor'=4] {'pop'}, dimensions={0}, use_global_device_ids=true | all-gather | bytes 681984 | tf_op jit(solution)/shard_map/all_gather | solution.py:73
  494.5 31.3 %all_gather.27 = bf16[64,3584]{1,0:T(8,128)(2,1)S(1)} all-gather(bf16[8,3584]{1,0:T(8,128)(2,1)S(1)} %copy-done.2), channel_id=1, replica_groups=mesh['pop'=8,'tensor'=4] {'pop'}, dimensions={0}, use_global_device_ids=true | all-gather | bytes 516096 | tf_op jit(solution)/shard_map/all_gather | solution.py:70
  525.8 40.9 %all_gather.29 = bf16[64,3584]{1,0:T(8,128)(2,1)S(1)} all-gather(bf16[8,3584]{1,0:T(8,128)(2,1)S(1)} %copy-done.3), channel_id=1, replica_groups=mesh['pop'=8,'tensor'=4] {'pop'}, dimensions={0}, use_global_device_ids=true | all-gather | bytes 516096 | tf_op jit(solution)/shard_map/all_gather | solution.py:71
  566.7 15.6 %all-to-all-start.1 = ((bf16[448,8,640]{2,0,1:T(8,128)(2,1)}), bf16[448,8,640]{2,0,1:T(8,128)(2,1)}, u32[]{:S(2)}, u32[]{:S(2)}) async-start(bf16[448,8,640]{2,0,1:T(8,128)(2,1)} %bitcast.38), calls=%async_computation.2 | async-start | bytes 9175040 | tf_op jit(solution)/shard_map/all_to_all | solution.py:58
  582.3 13.1 %fusion.11 = f32[64,1,64]{2,1,0:T(1,128)S(1)} fusion(bf16[64,64,3584]{2,1,0:T(8,128)(2,1)} %bitcast.48, bf16[64,3584,1]{1,0,2:T(8,128)(2,1)S(1)} %bitcast.44), kind=kOutput, calls=%fused_computation.18 | convolution fusion | flops 29360128 | bytes 29835264 | tf_op jit(solution)/shard_map/mld,md->ml/dot_general | solution.py:80
  595.4 13.1 %fusion.13 = f32[64,1,64]{2,1,0:T(1,128)S(1)} fusion(bf16[64,64,3584]{2,1,0:T(8,128)(2,1)} %bitcast.49, bf16[64,3584,1]{1,0,2:T(8,128)(2,1)S(1)} %bitcast.43), kind=kOutput, calls=%fused_computation.20 | convolution fusion | flops 29360128 | bytes 29835264 | tf_op jit(solution)/shard_map/mld,md->ml/dot_general | solution.py:80
  608.4 29.4 %fusion.27 = f32[64,64,640]{2,1,0:T(8,128)} fusion(bf16[64,64,3584]{2,1,0:T(8,128)(2,1)} %bitcast.50, bf16[3584,640,1]{1,0,2:T(8,128)(2,1)} %bitcast.4), kind=kOutput, calls=%fused_computation.53 | convolution fusion | flops 18790481920 | bytes 44433408 | tf_op jit(solution)/shard_map/dot_general | solution.py:79
  637.8 5.0 all-to-all-done.1
  642.8 30.8 %multiply_convert_fusion = bf16[64,64,640]{2,1,0:T(8,128)(2,1)} fusion(f32[64,64,640]{2,1,0:T(8,128)} %fusion.27, f32[64,640]{1,0:T(8,128)S(1)} %fusion.24, f32[64,64]{1,0:T(8,128)S(1)} %get-tuple-element.9, f32[64,640]{1,0:T(8,128)S(1)} %fusion.23, f32[64,64]{1,0:T(8,128)S(1)} %get-tuple-element.10, bf16[64,64,3584]{2,1,0:T(8,128)(2,1)} %bitcast.51, ...), kind=kOutput, calls=%fused_computation.1 | convolution fusion | flops 18816696320 | bytes 50036736 | tf_op jit(solution)/shard_map/dot_general | solution.py:79
  673.6 4.8 all-to-all-start.2
  679.9 97.4 %all-reduce.4 = s32[64]{0:T(128)S(1)} all-reduce(s32[64]{0:T(128)S(1)} %dynamic-update-slice), channel_id=1, replica_groups=mesh['pop'=8,'tensor'=4] {'pop'}, use_global_device_ids=true, to_apply=%add.4 | all-reduce | flops 64 | bytes 512
  777.5 4.7 fusion.7
  782.2 4.7 fusion.3
  786.9 3.3 copy.22
  (44 shorter events, 14.1 us)
Async XLA Ops:
  7.2 201.3 %reduce-scatter.2.cloned.1.call-start = ((), (), s32[]{:S(2)}) async-start(), calls=%async_computation.4 | async-start | bytes 8257536 | tf_op jit(solution)/shard_map/reduce_scatter | solution.py:55
  74.7 254.8 %all-gather.3.cloned.1.call-start = ((), (), s32[]{:S(2)}) async-start(), calls=%async_computation.5 | async-start | bytes 8257536 | tf_op jit(solution)/shard_map/all_gather | solution.py:66
  218.0 364.3 %all-gather.5.cloned.1.call-start = ((), (), s32[]{:S(2)}) async-start(), calls=%async_computation.6 | async-start | bytes 36700160 | tf_op jit(solution)/shard_map/all_gather | solution.py:67
  334.9 231.8 %all-to-all-start = ((bf16[448,8,640]{2,0,1:T(8,128)(2,1)}), bf16[448,8,640]{2,0,1:T(8,128)(2,1)}, u32[]{:S(2)}, u32[]{:S(2)}) async-start(bf16[448,8,640]{2,0,1:T(8,128)(2,1)} %bitcast.39), calls=%async_computation.1 | async-start | bytes 9175040 | tf_op jit(solution)/shard_map/all_to_all | solution.py:57
  339.7 7.2 copy-start
  343.7 119.0 %copy-start.1 = (bf16[8,4736]{1,0:T(8,128)(2,1)S(1)}, bf16[8,4736]{1,0:T(8,128)(2,1)}, u32[]{:S(2)}) copy-start(bf16[8,4736]{1,0:T(8,128)(2,1)} %param.19) | copy-start | bytes 227332
  343.7 150.8 %copy-start.2 = (bf16[8,3584]{1,0:T(8,128)(2,1)S(1)}, bf16[8,3584]{1,0:T(8,128)(2,1)}, u32[]{:S(2)}) copy-start(bf16[8,3584]{1,0:T(8,128)(2,1)} %param.16) | copy-start | bytes 172036
  343.7 182.1 %copy-start.3 = (bf16[8,3584]{1,0:T(8,128)(2,1)S(1)}, bf16[8,3584]{1,0:T(8,128)(2,1)}, u32[]{:S(2)}) copy-start(bf16[8,3584]{1,0:T(8,128)(2,1)} %param.17) | copy-start | bytes 172036
  566.7 76.1 %all-to-all-start.1 = ((bf16[448,8,640]{2,0,1:T(8,128)(2,1)}), bf16[448,8,640]{2,0,1:T(8,128)(2,1)}, u32[]{:S(2)}, u32[]{:S(2)}) async-start(bf16[448,8,640]{2,0,1:T(8,128)(2,1)} %bitcast.38), calls=%async_computation.2 | async-start | bytes 9175040 | tf_op jit(solution)/shard_map/all_to_all | solution.py:58
  673.6 4.8 copy-start.5
  673.6 6.1 copy-start.4
  673.6 113.3 %all-to-all-start.2 = ((bf16[8,512,640]{2,1,0:T(8,128)(2,1)}), bf16[8,512,640]{2,1,0:T(8,128)(2,1)}, u32[]{:S(2)}, u32[]{:S(2)}) async-start(bf16[8,512,640]{2,1,0:T(8,128)(2,1)} %bitcast.42), calls=%async_computation.3 | async-start | bytes 10485760 | tf_op jit(solution)/shard_map/all_to_all | solution.py:90
Sparse Core Ops, SparseCore 0:
  74.8 133.5 reduce-scatter.1
  218.1 111.3 all-gather.2
  331.1 175.9 all-gather.4
where the time goes:
time: 800 us; the launch traced here: 799 us
  blocking collectives  355 us (44%)
  waiting for transfers between devices  249 us (31%)
  matrix products  95.7 us (12%)
  local copies, waits for them, and re-layouts  47.3 us (6%)
  starting transfers between devices  25.3 us (3%)
  between operations  14.6 us (2%)
  other arithmetic  11.9 us (1%)
    reduce_scatter x1, waiting for transfers between devices, per_device(): lax.psum_scatter(partial_rows, 'pop', scatter_dimension=0, tiled=True)  133 us
    all_gather x1, blocking collectives, per_device(): lax.all_gather(gate_right, 'pop', axis=0, tiled=True)  116 us
    all_gather x1, waiting for transfers between devices, per_device(): some = lax.all_gather(own_normed, 'pop', axis=0, tiled=True)  111 us
    unnamed x1, blocking collectives  97.4 us
    dot_general x2, matrix products, project(): base = jnp.dot(normed, weight, preferred_element_type=jnp.float32)  60.2 us
    all_gather x1, blocking collectives, per_device(): lax.all_gather(up_left, 'pop', axis=0, tiled=True)  40.9 us
    all_gather x1, blocking collectives, per_device(): all_ids = lax.all_gather(token_ids, 'pop', axis=0, tiled=True)  32.3 us
    all_gather x1, blocking collectives, per_device(): lax.all_gather(up_right, 'pop', axis=0, tiled=True)  31.8 us
  transfers between devices with their start and end apart: 6, of which 3 were waited for; matrix products, arithmetic and copies ran while one was open for 10% of the time, Pallas kernels for 0%

commit v1 on v0

v1 whole, which is shorter than its diff:
```python
import math

import jax
import jax.numpy as jnp
from jax import lax
from jax.sharding import PartitionSpec as P


def split_high(x):
    high = lax.reduce_precision(x, exponent_bits=8, mantissa_bits=7)
    low = x - high
    return jnp.concatenate([high.astype(jnp.bfloat16), low.astype(jnp.bfloat16)], axis=0)


def weighted_step(left, right, score):
    scaled = split_high(left.astype(jnp.float32) * score[:, None])
    both = jnp.concatenate([right, right], axis=0)
    return lax.dot_general(
        scaled, both, (((0,), (0,)), ((), ())), preferred_element_type=jnp.float32
    )


def per_device(
    token_ids,
    ranks,
    embed_table,
    norm_gain,
    gate_weight,
    up_weight,
    gate_left,
    up_left,
    gate_right,
    up_right,
):
    pops = lax.axis_size("pop")
    pop = lax.axis_index("pop")
    tensor = lax.axis_index("tensor")
    table_rows, features = embed_table.shape
    own_members, prompt = token_ids.shape
    row_count, hidden_cols = gate_weight.shape
    width = norm_gain.shape[0]
    members = own_members * pops
    part = -(-hidden_cols // (128 * pops)) * 128
    padded = part * pops

    own_tokens = own_members * prompt
    cap = 2 * own_tokens // pops

    def pad_cols(x):
        return jnp.pad(x, ((0, 0), (0, padded - hidden_cols)))

    def exchange(x):
        return lax.all_to_all(x, "pop", 0, 0, tiled=True)

    def spread(x):
        return exchange(jnp.broadcast_to(x[None], (pops,) + x.shape))

    shared = spread(jnp.concatenate([token_ids.reshape(-1), ranks]))
    all_ids = shared[:, :own_tokens]
    all_ranks = shared[:, own_tokens:].reshape(-1)

    earlier = (
        jnp.arange(own_tokens)[:, None] < jnp.arange(own_tokens)[None, :]
    ).astype(jnp.bfloat16)

    def place(owned):
        return jnp.dot(
            owned.astype(jnp.bfloat16), earlier, preferred_element_type=jnp.float32
        ).astype(jnp.int32)

    local_ids = all_ids - pop * table_rows
    owned = (local_ids >= 0) & (local_ids < table_rows)
    slot = jnp.where(owned, place(owned), -1)
    wanted = jnp.sum(
        jnp.where(slot[:, None, :] == jnp.arange(cap)[None, :, None], local_ids[:, None, :], 0),
        axis=-1,
    )
    rows = jnp.take(embed_table, wanted.reshape(-1), axis=0, mode="clip")
    factors = jnp.concatenate(
        [
            jnp.broadcast_to(
                jnp.concatenate([gate_right, up_right], axis=1)[None],
                (pops, own_members, 2 * hidden_cols),
            ),
            gate_left.reshape(own_members, pops, row_count).transpose(1, 0, 2),
            up_left.reshape(own_members, pops, row_count).transpose(1, 0, 2),
        ],
        axis=2,
    )
    factors, _ = lax.optimization_barrier((factors, shared))
    factors = exchange(factors)
    rows, factors = lax.optimization_barrier((rows, factors))
    arrived = exchange(rows)

    def transposed(weight):
        return lax.all_to_all(weight, "pop", 1, 0, tiled=True)

    def gather(x, axis):
        return lax.all_gather(x, axis, axis=int(axis == "tensor"), tiled=True)

    ids = token_ids.reshape(-1)
    owner = ids // table_rows
    mine_of = owner[None, :] == jnp.arange(pops)[:, None]
    rank_in = jnp.sum(jnp.where(mine_of, place(mine_of), 0), axis=0)
    source = owner * cap + rank_in
    pick = (source[:, None] == jnp.arange(pops * cap)[None, :]).astype(jnp.bfloat16)
    values = jnp.dot(pick, arrived, preferred_element_type=jnp.float32)

    total = lax.psum(jnp.sum(values * values, axis=-1), "tensor")
    gain = lax.dynamic_slice_in_dim(norm_gain, tensor * features, features, 0)
    own_normed = (
        values * lax.rsqrt(total[:, None] * (1.0 / width) + 1e-06) * gain.astype(jnp.float32)
    ).astype(jnp.bfloat16)

    def own_side(left):
        cols = lax.dynamic_slice_in_dim(left, tensor * features, features, 1)
        return jnp.sum(
            own_normed.astype(jnp.float32).reshape(own_members, prompt, features)
            * cols.astype(jnp.float32)[:, None, :],
            axis=-1,
        )

    scale = 0.5 / math.sqrt(width)
    sides = lax.psum(jnp.stack([own_side(gate_left), own_side(up_left)]), "tensor") * scale

    first = own_members * 5 // 8
    split = first * prompt
    gate_in, up_in = pad_cols(gate_weight), pad_cols(up_weight)
    own_normed, sides, gate_in, up_in = lax.optimization_barrier(
        (own_normed, sides, gate_in, up_in)
    )
    some1 = gather(own_normed[:split], "pop")
    gate_cols = transposed(gate_in)
    some1, gate_cols, up_in = lax.optimization_barrier((some1, gate_cols, up_in))
    normed1 = gather(some1, "tensor")
    up_cols = transposed(up_in)
    normed1, up_cols, own_rest, sides = lax.optimization_barrier(
        (normed1, up_cols, own_normed[split:], sides)
    )
    some2 = gather(own_rest, "pop")
    sides = spread(sides).reshape(pops, 2, own_members, prompt)
    factors = factors.reshape(members, 2 * (hidden_cols + row_count))
    all_gr = factors[:, :hidden_cols]
    all_ur = factors[:, hidden_cols : 2 * hidden_cols]
    left_gate = factors[:, 2 * hidden_cols : 2 * hidden_cols + row_count]
    left_up = factors[:, 2 * hidden_cols + row_count :]

    def right_cols(right):
        cols = lax.dynamic_slice_in_dim(pad_cols(right), pop * part, part, 1)
        return cols.astype(jnp.float32).reshape(pops, own_members, part)

    gate_right_cols = right_cols(all_gr)
    up_right_cols = right_cols(all_ur)

    def project(normed, weight, side, cols, lo, hi):
        base = jnp.dot(normed, weight, preferred_element_type=jnp.float32)
        return (
            base.reshape(pops, hi - lo, prompt, part)
            + side[:, lo:hi, :, None] * cols[:, lo:hi, None, :]
        )

    def activate(normed, lo, hi):
        gate = project(normed, gate_cols, sides[:, 0], gate_right_cols, lo, hi)
        up = project(normed, up_cols, sides[:, 1], up_right_cols, lo, hi)
        mine = (jax.nn.silu(gate) * up).astype(jnp.bfloat16)
        return mine.reshape(pops * (hi - lo) * prompt, part)

    def send_home(mine):
        return lax.all_to_all(mine, "pop", 0, 1, tiled=True)[:, :hidden_cols]

    mine1 = activate(normed1, 0, first)
    mine1, some2 = lax.optimization_barrier((mine1, some2))
    normed2 = gather(some2, "tensor")
    home1 = send_home(mine1)
    home2 = send_home(activate(normed2, first, own_members))
    pieces = [home1, home2]
    hidden = jnp.concatenate(pieces, axis=0)

    score = (2.0 * all_ranks.astype(jnp.float32) - (members - 1)) / (members - 1)
    score = score * (1.0 / math.sqrt(members))
    gate_step = weighted_step(left_gate, all_gr, score)
    up_step = weighted_step(left_up, all_ur, score)
    return (hidden, gate_step, up_step)


def solution(mesh):
    in_specs = (
        P("pop", None),
        P("pop"),
        P("pop", "tensor"),
        P(),
        P("pop", "tensor"),
        P("pop", "tensor"),
        P("pop", None),
        P("pop", None),
        P("pop", "tensor"),
        P("pop", "tensor"),
    )
    out_specs = (P("pop", "tensor"), P("pop", "tensor"), P("pop", "tensor"))
    return jax.shard_map(
        per_device, mesh=mesh, in_specs=in_specs, out_specs=out_specs, check_vma=False
    )
```

time: 800 us -> 626 us (0.78)
  blocking collectives: 355 us -> 12.4 us
  waiting for transfers between devices: 249 us -> 413 us
  starting transfers between devices: 25.3 us -> 39.7 us
  matrix products: 95.7 us -> 85.5 us
    all_to_all x3 -> x8, waiting for transfers between devices: 5.01 us -> 338 us  [the longest x2 255 us: transposed(): return lax.all_to_all(weight, 'pop', 1, 0, tiled=True)]
    all_gather x5 -> x0, blocking collectives: 252 us -> none  [the longest x1 116 us: per_device(): lax.all_gather(gate_right, 'pop', axis=0, tiled=True)]
    reduce_scatter x1 -> x0, waiting for transfers between devices: 133 us -> none  [per_device(): lax.psum_scatter(partial_rows, 'pop', scatter_dimension=0, tiled=True)]
    unnamed x1 -> x0, blocking collectives: 97.4 us -> none
    all_gather x2 -> x4, waiting for transfers between devices: 111 us -> 74.6 us  [gather(): return lax.all_gather(x, axis, axis=int(axis == 'tensor'), tiled=True)]
    dot_general x2 -> x3, matrix products: 26.1 us -> 2.9 us  [the longest x1 2.53 us: per_device(): values = jnp.dot(pick, arrived, preferred_element_type=jnp.float32)]
    all_to_all x3 -> x8, starting transfers between devices: 25.1 us -> 39.4 us  [the longest x4 20.6 us: exchange(): return lax.all_to_all(x, 'pop', 0, 0, tiled=True)]
    gather x1, local copies, waits for them, and re-layouts: 27.8 us -> 13.8 us  [per_device(): rows = jnp.take(embed_table, wanted.reshape(-1), axis=0, mode='clip')]
  transfers between devices with their start and end apart: 6 -> 12, of which waited for: 3 -> 9; matrix products, arithmetic and copies ran while one was open for 10% -> 20% of each run, Pallas kernels for 0% -> 0%
where the time goes in v1:
time: 626 us; the launch traced here: 624 us
  waiting for transfers between devices  413 us (66%)
  matrix products  85.5 us (14%)
  local copies, waits for them, and re-layouts  49.7 us (8%)
  starting transfers between devices  39.7 us (6%)
  between operations  14 us (2%)
  blocking collectives  12.4 us (2%)
  other arithmetic  9.9 us (2%)
    all_to_all x2, waiting for transfers between devices, transposed(): return lax.all_to_all(weight, 'pop', 1, 0, tiled=True)  255 us
    all_gather x4, waiting for transfers between devices, gather(): return lax.all_gather(x, axis, axis=int(axis == 'tensor'), tiled=True)  74.6 us
    dot_general x4, matrix products, project(): base = jnp.dot(normed, weight, preferred_element_type=jnp.float32)  71.8 us
    all_to_all x4, waiting for transfers between devices, exchange(): return lax.all_to_all(x, 'pop', 0, 0, tiled=True)  49.8 us
    all_to_all x2, waiting for transfers between devices, send_home(): return lax.all_to_all(mine, 'pop', 0, 1, tiled=True)[:, :hidden_cols]  33.3 us
    all_to_all x4, starting transfers between devices, exchange(): return lax.all_to_all(x, 'pop', 0, 0, tiled=True)  20.6 us
    gather x1, local copies, waits for them, and re-layouts, per_device(): rows = jnp.take(embed_table, wanted.reshape(-1), axis=0, mode='clip')  13.8 us
  transfers between devices with their start and end apart: 12, of which 9 were waited for; matrix products, arithmetic and copies ran while one was open for 20% of the time, Pallas kernels for 0%

profile of v1, /device:TPU:0, one launch (start us, length us, event | category | flops | bytes accessed | tf_op | source)
XLA Modules:
  0.0 624.3 jit_solution(15834536692148445228)
XLA Ops:
  9.2 7.3 %all-to-all-start = ((s32[8,1,520]{2,1,0:T(1,128)}), s32[8,1,520]{2,1,0:T(1,128)S(1)}, u32[]{:S(2)}, u32[]{:S(2)}) async-start(s32[8,1,520]{2,1,0:T(1,128)} %broadcast_in_dim.30), calls=%async_computation | async-start | bytes 40960 | tf_op jit(solution)/shard_map/all_to_all | solution.py:53
  27.8 13.8 %gather_fusion = bf16[1024,896]{1,0:T(8,128)(2,1)} fusion(bf16[9504,896]{1,0:T(8,128)(2,1)} %param.12, s32[1024]{0:T(1024)S(1)} %bitcast_clamp_fusion), kind=kCustom, calls=%fused_computation | custom fusion | bytes 3674112 | tf_op jit(solution)/shard_map/jit(_take)/gather | solution.py:78
  41.6 17.0 %all-to-all-done.1 = bf16[8,8,10368]{2,1,0:T(8,128)(2,1)S(1)} async-done(((bf16[8,8,10368]{2,1,0:T(8,128)(2,1)}), bf16[8,8,10368]{2,1,0:T(8,128)(2,1)S(1)}, u32[]{:S(2)}, u32[]{:S(2)}) %all-to-all-start.1) | async-done | bytes 1327136 | tf_op jit(solution)/shard_map/all_to_all | solution.py:53
  62.2 4.9 pad.14
  67.2 4.9 pad.15
  73.9 31.1 %all-to-all-done.2 = bf16[8,128,896]{2,1,0:T(8,128)(2,1)S(1)} async-done(((bf16[8,128,896]{2,1,0:T(8,128)(2,1)}), bf16[8,128,896]{2,1,0:T(8,128)(2,1)S(1)}, u32[]{:S(2)}, u32[]{:S(2)}) %all-to-all-start.2) | async-done | bytes 1835040 | tf_op jit(solution)/shard_map/all_to_all | solution.py:53
  107.5 5.6 psum.14
  115.4 6.7 %psum.15 = f32[2,8,64]{2,1,0:T(8,128)S(1)} all-reduce(f32[2,8,64]{2,1,0:T(8,128)S(1)} %pad_maximum_fusion.2), channel_id=1, replica_groups=mesh['pop'=8,'tensor'=4] {'tensor'}, use_global_device_ids=true, to_apply=%region_6.7 | all-reduce | flops 1024 | bytes 8192 | tf_op jit(solution)/shard_map/psum | solution.py:124
  122.1 4.9 copy.48
  132.6 155.5 %all-to-all-done.3 = bf16[448,8,640]{2,0,1:T(8,128)(2,1)} async-done(((bf16[448,8,640]{2,0,1:T(8,128)(2,1)}), bf16[448,8,640]{2,0,1:T(8,128)(2,1)}, u32[]{:S(2)}, u32[]{:S(2)}) %all-to-all-start.3) | async-done | bytes 4587552 | tf_op jit(solution)/shard_map/all_to_all | solution.py:96
  288.2 4.9 copy.47
  293.1 4.7 all-to-all-start.4
  298.6 99.8 %all-to-all-done.4 = bf16[448,8,640]{2,0,1:T(8,128)(2,1)} async-done(((bf16[448,8,640]{2,0,1:T(8,128)(2,1)}), bf16[448,8,640]{2,0,1:T(8,128)(2,1)}, u32[]{:S(2)}, u32[]{:S(2)}) %all-to-all-start.4) | async-done | bytes 4587552 | tf_op jit(solution)/shard_map/all_to_all | solution.py:96
  398.4 5.9 all-gather.7.cloned.1.call-done
  407.6 5.5 all-to-all-start.5
  413.3 20.0 %fusion.48 = f32[2560,640]{1,0:T(8,128)} fusion(bf16[2560,3584]{1,0:T(8,128)(2,1)} %all-gather.7.cloned.1.call-done, bf16[3584,640]{1,0:T(8,128)(2,1)} %bitcast.8), kind=kOutput, calls=%fused_computation.94 | convolution fusion | flops 11744051200 | bytes 29491200 | tf_op jit(solution)/shard_map/dot_general | solution.py:156
  434.8 25.8 %fusion.2 = bf16[2560,640]{1,0:T(8,128)(2,1)} fusion(f32[2560,640]{1,0:T(8,128)} %fusion.48, bf16[2560,3584]{1,0:T(8,128)(2,1)} %all-gather.7.cloned.1.call-done, bf16[3584,640]{1,0:T(8,128)(2,1)} %bitcast.10, f32[8,5,640]{2,1,0:T(8,128)S(1)} %bitcast.103, f32[2560]{0:T(1024)S(1)} %mul.230, f32[8,5,640]{2,1,0:T(8,128)S(1)} %bitcast.102, f32[2560]{0:T(1024)S(1)} %mul.223), kind=kOutput, calls=%fused_computation.4 | convolution fusion | flops 11760435200 | bytes 32993280 | tf_op jit(solution)/shard_map/dot_general | solution.py:156
  468.9 66.8 %all-gather.11.cloned.1.call-done = bf16[1536,3584]{1,0:T(8,128)(2,1)} async-done(((bf16[1536,896]{1,0:T(8,128)(2,1)}), bf16[1536,3584]{1,0:T(8,128)(2,1)}) %all-gather.11.cloned.1.call-update) | async-done | bytes 11010064 | tf_op jit(solution)/shard_map/all_gather | solution.py:99
  535.7 12.9 %fusion.49 = f32[1536,640]{1,0:T(8,128)S(1)} fusion(bf16[1536,3584]{1,0:T(8,128)(2,1)} %all-gather.11.cloned.1.call-done, bf16[3584,640]{1,0:T(8,128)(2,1)} %bitcast.8), kind=kOutput, calls=%fused_computation.95 | convolution fusion | flops 7046430720 | bytes 19529728 | tf_op jit(solution)/shard_map/dot_general | solution.py:156
  548.6 13.1 %fusion.6 = bf16[1536,640]{1,0:T(8,128)(2,1)} fusion(f32[1536,640]{1,0:T(8,128)S(1)} %fusion.49, bf16[1536,3584]{1,0:T(8,128)(2,1)S(1)} %copy-done.6, bf16[3584,640]{1,0:T(8,128)(2,1)} %bitcast.10, f32[8,3,640]{2,1,0:T(4,128)S(1)} %copy-done.4, f32[1536]{0:T(1024)S(1)} %mul.242, f32[8,3,640]{2,1,0:T(4,128)S(1)} %copy-done.5, f32[1536]{0:T(1024)S(1)} %mul.236), kind=kOutput, calls=%fused_computation.13 | convolution fusion | flops 7056261120 | bytes 21630976 | tf_op jit(solution)/shard_map/dot_general | solution.py:156
  561.7 5.5 all-to-all-start.7
  568.4 6.0 fusion.15
  574.4 4.7 fusion.11
  579.9 33.3 %all-to-all-done.7 = bf16[8,192,640]{2,1,0:T(8,128)(2,1)} async-done(((bf16[8,192,640]{2,1,0:T(8,128)(2,1)}), bf16[8,192,640]{2,1,0:T(8,128)(2,1)}, u32[]{:S(2)}, u32[]{:S(2)}) %all-to-all-start.7) | async-done | bytes 1966112 | tf_op jit(solution)/shard_map/all_to_all | solution.py:169
  (86 shorter events, 49.5 us)
Async XLA Ops:
  9.2 13.9 %all-to-all-start = ((s32[8,1,520]{2,1,0:T(1,128)}), s32[8,1,520]{2,1,0:T(1,128)S(1)}, u32[]{:S(2)}, u32[]{:S(2)}) async-start(s32[8,1,520]{2,1,0:T(1,128)} %broadcast_in_dim.30), calls=%async_computation | async-start | bytes 40960 | tf_op jit(solution)/shard_map/all_to_all | solution.py:53
  23.1 35.6 %all-to-all-start.1 = ((bf16[8,8,10368]{2,1,0:T(8,128)(2,1)}), bf16[8,8,10368]{2,1,0:T(8,128)(2,1)S(1)}, u32[]{:S(2)}, u32[]{:S(2)}) async-start(bf16[8,8,10368]{2,1,0:T(8,128)(2,1)} %concatenate.26), calls=%async_computation.1 | async-start | bytes 2654208 | tf_op jit(solution)/shard_map/all_to_all | solution.py:53
  58.6 346.4 %copy-start = (bf16[8,8,10368]{2,1,0:T(8,128)(2,1)}, bf16[8,8,10368]{2,1,0:T(8,128)(2,1)S(1)}, u32[]{:S(2)}) copy-start(bf16[8,8,10368]{2,1,0:T(8,128)(2,1)S(1)} %all-to-all-done.1) | copy-start | bytes 3981316
  58.6 46.3 %all-to-all-start.2 = ((bf16[8,128,896]{2,1,0:T(8,128)(2,1)}), bf16[8,128,896]{2,1,0:T(8,128)(2,1)S(1)}, u32[]{:S(2)}, u32[]{:S(2)}) async-start(bf16[8,128,896]{2,1,0:T(8,128)(2,1)} %bitcast.3), calls=%async_computation.2 | async-start | bytes 3670016 | tf_op jit(solution)/shard_map/all_to_all | solution.py:53
  127.0 161.1 %all-to-all-start.3 = ((bf16[448,8,640]{2,0,1:T(8,128)(2,1)}), bf16[448,8,640]{2,0,1:T(8,128)(2,1)}, u32[]{:S(2)}, u32[]{:S(2)}) async-start(bf16[448,8,640]{2,0,1:T(8,128)(2,1)} %bitcast.91), calls=%async_computation.3 | async-start | bytes 9175040 | tf_op jit(solution)/shard_map/all_to_all | solution.py:96
  131.6 156.5 %all-gather.5.cloned.1.call-start = ((), (), s32[]{:S(2)}) async-start(), calls=%async_computation.8 | async-start | bytes 5160960 | tf_op jit(solution)/shard_map/all_gather | solution.py:99
  132.6 271.7 %all-gather.7.cloned.1.call-start = ((), (), s32[]{:S(2)}) async-start(), calls=%async_computation.9 | async-start | bytes 22937600 | tf_op jit(solution)/shard_map/all_gather | solution.py:99
  293.1 105.3 %all-to-all-start.4 = ((bf16[448,8,640]{2,0,1:T(8,128)(2,1)}), bf16[448,8,640]{2,0,1:T(8,128)(2,1)}, u32[]{:S(2)}, u32[]{:S(2)}) async-start(bf16[448,8,640]{2,0,1:T(8,128)(2,1)} %bitcast.92), calls=%async_computation.4 | async-start | bytes 9175040 | tf_op jit(solution)/shard_map/all_to_all | solution.py:96
  297.8 164.7 %all-gather.9.cloned.1.call-start = ((), (), s32[]{:S(2)}) async-start(), calls=%async_computation.10 | async-start | bytes 3096576 | tf_op jit(solution)/shard_map/all_gather | solution.py:99
  406.0 0.8 copy-start.1
  406.8 27.9 %copy-start.3 = (f32[8,8,640]{2,1,0:T(8,128)}, f32[8,8,640]{2,1,0:T(8,128)S(1)}, u32[]{:S(2)}) copy-start(f32[8,8,640]{2,1,0:T(8,128)S(1)} %get-tuple-element.51) | copy-start | bytes 491524
  407.6 25.7 %all-to-all-start.5 = ((f32[8,1,1024]{2,1,0:T(1,128)}), f32[8,1,1024]{2,1,0:T(1,128)S(1)}, u32[]{:S(2)}, u32[]{:S(2)}) async-start(f32[8,1,1024]{2,1,0:T(1,128)} %reshape.175), calls=%async_computation.5 | async-start | bytes 65536 | tf_op jit(solution)/shard_map/all_to_all | solution.py:53
  413.1 122.6 %all-gather.11.cloned.1.call-start = ((), (), s32[]{:S(2)}) async-start(), calls=%async_computation.11 | async-start | bytes 13762560 | tf_op jit(solution)/shard_map/all_gather | solution.py:99
  462.5 99.2 %all-to-all-start.6 = ((bf16[8,320,640]{2,1,0:T(8,128)(2,1)}), bf16[8,320,640]{2,1,0:T(8,128)(2,1)S(1)}, u32[]{:S(2)}, u32[]{:S(2)}) async-start(bf16[8,320,640]{2,1,0:T(8,128)(2,1)} %bitcast.99), calls=%async_computation.6 | async-start | bytes 6553600 | tf_op jit(solution)/shard_map/all_to_all | solution.py:169
  468.9 79.7 %copy-start.4 = (f32[8,3,640]{2,1,0:T(4,128)S(1)}, f32[8,3,640]{2,1,0:T(4,128)}, u32[]{:S(2)}) copy-start(f32[8,3,640]{2,1,0:T(4,128)} %slice.101) | copy-start | bytes 184324
  468.9 79.7 %copy-start.5 = (f32[8,3,640]{2,1,0:T(4,128)S(1)}, f32[8,3,640]{2,1,0:T(4,128)}, u32[]{:S(2)}) copy-start(f32[8,3,640]{2,1,0:T(4,128)} %slice.99) | copy-start | bytes 184324
  535.7 13.0 %copy-start.6 = (bf16[1536,3584]{1,0:T(8,128)(2,1)S(1)}, bf16[1536,3584]{1,0:T(8,128)(2,1)}, u32[]{:S(2)}) copy-start(bf16[1536,3584]{1,0:T(8,128)(2,1)} %all-gather.11.cloned.1.call-done) | copy-start | bytes 33030148
  561.7 51.5 %all-to-all-start.7 = ((bf16[8,192,640]{2,1,0:T(8,128)(2,1)}), bf16[8,192,640]{2,1,0:T(8,128)(2,1)}, u32[]{:S(2)}, u32[]{:S(2)}) async-start(bf16[8,192,640]{2,1,0:T(8,128)(2,1)} %bitcast.100), calls=%async_computation.7 | async-start | bytes 3932160 | tf_op jit(solution)/shard_map/all_to_all | solution.py:169
  568.3 6.1 copy-start.2
Sparse Core Ops, SparseCore 0:
  135.2 148.2 all-gather.4
  288.3 115.8 all-gather.6
  406.4 56.0 all-gather.8
  463.9 71.7 all-gather.10
